TPU v7x, 1024 devices: a whole 8x8x8 slice. The times are simulated.
1024 devices in a mesh: pair: 64 (over x, z), virt: 16 (over y, core).
Axes of the slice: x: 8, y: 8, z: 8, core: 2. Of those that a mesh axis runs over, the one named last changes fastest.
Arguments:
- amplitudes: bfloat16 [4096, 128, 128], P('pair'), as said below
- factors: bfloat16 [64, 128, 128], P(None, 'virt'), may hold values from -0.1875 to 0.1875
- ov_factors: bfloat16 [64, 64, 128], replicated, may hold values from -0.15625 to 0.15625
- fock_matrix: bfloat16 [128, 128], replicated, may hold values from -0.5 to 0.5
- screen: int32 [64, 64], P('pair'), may hold values 0 or 1
Outputs:
- residual: bfloat16 [4096, 128, 128], P('pair', 'virt')
Inputs may be any that keep to these rules, and one draw needn't show every extreme that they name: amplitudes[(j,i), c, d] = amplitudes[(i,j), d, c] for all pairs.
All inputs are finite; a program needn't handle non-finite values. No bound on the sum of `screen` on one device may be relied on, other than what follows from the above.
Results may differ from a plain program's by a relative error of at most 0.0095.
Values may be sent and summed in bfloat16 or wider, within the bound.
A program may use at most 32 MiB of HBM per device.

v0:
```python
import jax
import jax.numpy as jnp
from jax import lax
from jax.sharding import PartitionSpec as P


def body(amplitudes, factors, ov_factors, fock_matrix, screen):
    row_count = amplitudes.shape[0]
    virt_width = amplitudes.shape[1]
    pair_count = lax.axis_size("pair")
    virt_count = lax.axis_size("virt")
    local_width = virt_width // virt_count
    offset = lax.axis_index("virt") * local_width
    intermediate = jnp.einsum(
        "pcd,qbd->pqbc", amplitudes, factors, preferred_element_type=jnp.float32
    ).astype(jnp.bfloat16)
    ladder = jnp.einsum(
        "qac,pqbc->pba",
        lax.all_gather(factors, "virt", axis=1, tiled=True),
        intermediate,
        preferred_element_type=jnp.float32,
    ).astype(jnp.bfloat16)
    occ_count = row_count // pair_count
    occ_total = ov_factors.shape[1]
    amp_grid = amplitudes.reshape(occ_count, occ_total, virt_width, virt_width)
    dressed = 2.0 * jnp.einsum(
        "xkac,pkc->xap", amp_grid, ov_factors, preferred_element_type=jnp.float32
    )
    dressed = dressed - jnp.einsum(
        "xkca,pkc->xap", amp_grid, ov_factors, preferred_element_type=jnp.float32
    )
    dressed = dressed.astype(jnp.bfloat16)
    ov_cols = lax.dynamic_slice_in_dim(ov_factors, offset, local_width, 2)
    cycle = jnp.einsum(
        "xap,pjb->xjba", dressed, ov_cols, preferred_element_type=jnp.float32
    ).astype(jnp.bfloat16)
    cycle = cycle.reshape(row_count, local_width, virt_width)
    outgoing = cycle.reshape(occ_count, pair_count, occ_count, local_width, virt_width).transpose(
        1, 0, 2, 3, 4
    )
    incoming = lax.all_to_all(
        lax.all_to_all(outgoing, "pair", split_axis=0, concat_axis=0, tiled=True),
        "virt",
        split_axis=4,
        concat_axis=3,
        tiled=True,
    )
    mirror = incoming.transpose(2, 0, 1, 4, 3).reshape(row_count, local_width, virt_width)
    fock_cols = lax.dynamic_slice_in_dim(fock_matrix, offset, local_width, 1)
    amp_cols = lax.dynamic_slice_in_dim(amplitudes, offset, local_width, 2)
    fock_term = jnp.einsum("pac,cb->pba", amplitudes, fock_cols, preferred_element_type=jnp.float32)
    fock_term = fock_term + jnp.einsum(
        "ac,pcb->pba", fock_matrix, amp_cols, preferred_element_type=jnp.float32
    )
    weight = screen.reshape(row_count).astype(jnp.float32)[:, None, None]
    total = weight * (
        ladder.astype(jnp.float32)
        + cycle.astype(jnp.float32)
        + mirror.astype(jnp.float32)
        + fock_term
    )
    return total.astype(jnp.bfloat16)


def solution(mesh):
    in_specs = (P("pair", None, None), P(None, "virt", None), P(), P(), P("pair", None))
    out_specs = P("pair", "virt", None)
    return jax.shard_map(body, mesh=mesh, in_specs=in_specs, out_specs=out_specs, check_vma=False)
```

profile of v0, /device:TPU:1, one launch (start us, length us, event | category | flops | bytes accessed | tf_op | source)
XLA Modules:
  0.0 86.4 jit_solution(10316659478768116054)
XLA Ops:
  6.5 0.0 copy-start
  6.5 0.0 copy-start.1
  6.5 0.0 all-gather.2.cloned.1.call-start
  6.5 0.7 all-gather.2.cloned.1.call-update
  7.3 2.8 %constant_dynamic-slice_fusion = bf16[64,64,8]{2,1,0:T(8,128)(2,1)} fusion(bf16[64,64,128]{2,1,0:T(8,128)(2,1)} %param.7, s32[]{:T(128)S(6)} %select_n.2), kind=kLoop, calls=%fused_computation.35 | loop fusion | bytes 131076 | tf_op jit(solution)/shard_map/dynamic_slice | solution.py:33
  10.1 0.0 copy-done
  10.1 0.0 copy-done.1
  10.1 0.8 fusion.58
  10.8 0.0 copy-start.2
  10.8 2.6 %convolution_convert_fusion = bf16[64,8,128]{2,1,0:T(8,128)(2,1)S(1)} fusion(bf16[64,64,8]{2,1,0:T(8,128)(2,1)} %constant_dynamic-slice_fusion, f32[128,64]{0,1:T(8,128)S(1)} %fusion.58, bf16[64,128,128]{2,1,0:T(8,128)(2,1)S(1)} %copy-done, bf16[64,64,128]{2,1,0:T(8,128)(2,1)S(1)} %copy-done.1), kind=kOutput, calls=%fused_computation.14 | convolution fusion | flops 142688256 | bytes 3375104 | tf_op jit(solution)/shard_map/xap,pjb->xjba/dot_general | solution.py:34
  13.5 0.0 copy-start.4
  13.5 34.5 %all_to_all.17 = bf16[64,1,1,8,128]{4,3,2,1,0:T(8,128)(2,1)S(1)} all-to-all(bf16[64,1,1,8,128]{4,3,2,1,0:T(8,128)(2,1)S(1)} %bitcast.107), channel_id=1, replica_groups=mesh['pair'=64,'virt'=16] {'pair'}, dimensions={0} | all-to-all | bytes 262144 | tf_op jit(solution)/shard_map/all_to_all | solution.py:42
  48.0 0.2 copy.30
  48.2 0.9 %reshape.42 = bf16[16,2,2048]{2,1,0:T(2,128)(2,1)} reshape(bf16[128,1,1,8,64]{4,3,2,1,0:T(8,128)(2,1)S(1)} %bitcast.106) | data formatting | bytes 262144
  49.1 9.7 %all-to-all-start.1 = ((bf16[16,2,2048]{2,1,0:T(2,128)(2,1)}), bf16[16,2,2048]{2,1,0:T(2,128)(2,1)S(1)}, u32[]{:S(2)}, u32[]{:S(2)}) async-start(bf16[16,2,2048]{2,1,0:T(2,128)(2,1)} %reshape.42), calls=%async_computation.1 | async-start | bytes 262144 | tf_op jit(solution)/shard_map/all_to_all | solution.py:41
  58.8 0.0 copy-done.2
  58.8 0.7 convolution_bitcast_fusion
  59.5 0.0 copy-done.4
  59.6 0.0 copy-start.3
  59.6 7.9 %all-to-all-done.1 = bf16[16,2,2048]{2,1,0:T(2,128)(2,1)S(1)} async-done(((bf16[16,2,2048]{2,1,0:T(2,128)(2,1)}), bf16[16,2,2048]{2,1,0:T(2,128)(2,1)S(1)}, u32[]{:S(2)}, u32[]{:S(2)}) %all-to-all-start.1) | async-done | bytes 131104 | tf_op jit(solution)/shard_map/all_to_all | solution.py:41
  67.4 0.2 reshape.43
  67.7 0.2 copy.33
  68.0 2.9 %all-gather.2.cloned.1.call-done = bf16[64,128,128]{2,1,0:T(8,128)(2,1)} async-done(((bf16[64,8,128]{2,1,0:T(8,128)(2,1)}), bf16[64,128,128]{2,1,0:T(8,128)(2,1)}) %all-gather.2.cloned.1.call-update) | async-done | bytes 2097168 | tf_op jit(solution)/shard_map/all_gather | solution.py:19
  70.9 0.0 copy-done.3
  70.9 6.1 %fusion.50 = f32[64,8,128]{2,1,0:T(8,128)S(1)} fusion(bf16[64,128,128]{2,1,0:T(8,128)(2,1)} %all-gather.2.cloned.1.call-done, bf16[64,128,128]{2,1,0:T(8,128)(2,1)S(1)} %copy-done, f32[64,1,1,128,8]{3,4,0,1,2:T(8,128)S(1)} %copy.33, bf16[64,8,128]{2,1,0:T(8,128)(2,1)S(1)} %convolution_convert_fusion, bf16[64,8,128]{2,1,0:T(8,128)(2,1)S(1)} %copy-done.3), kind=kOutput, calls=%fused_computation.18 | convolution fusion | flops 2152005632 | bytes 4980736 | tf_op jit(solution)/shard_map/qac,pqbc->pba/dot_general | solution.py:17
  77.0 2.5 %fusion.26 = bf16[64,8,128]{2,1,0:T(8,128)(2,1)} fusion(f32[64,8,128]{2,1,0:T(8,128)S(1)} %fusion.50, f32[64,8,128]{2,1,0:T(8,128)S(1)} %convolution_bitcast_fusion, bf16[64,128,128]{2,1,0:T(8,128)(2,1)S(1)} %copy-done, s32[]{:T(128)S(6)} %select_n.2, f32[64]{0:T(128)S(1)} %convert_bitcast_fusion.1, bf16[128,128]{1,0:T(8,128)(2,1)S(1)} %copy-done.2), kind=kOutput, calls=%fused_computation.13 | convolution fusion | flops 17039360 | bytes 2785540 | tf_op jit(solution)/shard_map/ac,pcb->pba/dot_general | solution.py:52
  (3 shorter events, 0.1 us)
Async XLA Ops:
  6.5 3.5 %copy-start = (bf16[64,128,128]{2,1,0:T(8,128)(2,1)S(1)}, bf16[64,128,128]{2,1,0:T(8,128)(2,1)}, u32[]{:S(2)}) copy-start(bf16[64,128,128]{2,1,0:T(8,128)(2,1)} %param.5) | copy-start | bytes 6291460
  6.5 3.5 %copy-start.1 = (bf16[64,64,128]{2,1,0:T(8,128)(2,1)S(1)}, bf16[64,64,128]{2,1,0:T(8,128)(2,1)}, u32[]{:S(2)}) copy-start(bf16[64,64,128]{2,1,0:T(8,128)(2,1)} %param.7) | copy-start | bytes 3145732
  6.5 64.4 %all-gather.2.cloned.1.call-start = ((), (), s32[]{:S(2)}) async-start(), calls=%async_computation.2 | async-start | bytes 2228224 | tf_op jit(solution)/shard_map/all_gather | solution.py:19
  10.8 48.0 %copy-start.2 = (bf16[128,128]{1,0:T(8,128)(2,1)S(1)}, bf16[128,128]{1,0:T(8,128)(2,1)}, u32[]{:S(2)}) copy-start(bf16[128,128]{1,0:T(8,128)(2,1)} %param.8) | copy-start | bytes 98308
  13.5 46.1 %copy-start.4 = (s32[1,64]{1,0:T(1,128)S(1)}, s32[1,64]{1,0:T(1,128)}, u32[]{:S(2)}) copy-start(s32[1,64]{1,0:T(1,128)} %param.9) | copy-start | bytes 772
  49.1 18.4 %all-to-all-start.1 = ((bf16[16,2,2048]{2,1,0:T(2,128)(2,1)}), bf16[16,2,2048]{2,1,0:T(2,128)(2,1)S(1)}, u32[]{:S(2)}, u32[]{:S(2)}) async-start(bf16[16,2,2048]{2,1,0:T(2,128)(2,1)} %reshape.42), calls=%async_computation.1 | async-start | bytes 262144 | tf_op jit(solution)/shard_map/all_to_all | solution.py:41
  59.6 11.4 %copy-start.3 = (bf16[64,8,128]{2,1,0:T(8,128)(2,1)S(1)}, bf16[64,8,128]{2,1,0:T(8,128)(2,1)}, u32[]{:S(2)}) copy-start(bf16[64,8,128]{2,1,0:T(8,128)(2,1)} %param.6) | copy-start | bytes 393220
Sparse Core Ops, SparseCore 0:
  10.0 60.8 all-gather.1
where the time goes:
time: 86.6 us; the launch traced here: 86.4 us
  blocking collectives  34.5 us (40%)
  between operations  13.5 us (16%)
  matrix products  12.7 us (15%)
  waiting for transfers between devices  11.5 us (13%)
  starting transfers between devices  9.74 us (11%)
  local copies, waits for them, and re-layouts  4.42 us (5%)
    all_to_all x1, blocking collectives, body(): lax.all_to_all(outgoing, 'pair', split_axis=0, concat_axis=0, tiled=True)  34.5 us
    all_to_all x1, starting transfers between devices, body(): lax.all_to_all(lax.all_to_all(outgoing, 'pair', split_axis=0, concat_axis...  9.73 us
    all_to_all x1, waiting for transfers between devices, body(): lax.all_to_all(lax.all_to_all(outgoing, 'pair', split_axis=0, concat_axis...  7.88 us
    dot_general x1, matrix products, body(): jnp.einsum('qac,pqbc->pba', lax.all_gather(factors, 'virt', axis=1, tiled...  6.09 us
    all_gather x1, waiting for transfers between devices, body(): lax.all_gather(factors, 'virt', axis=1, tiled=True)  2.92 us
    dynamic_slice x1, local copies, waits for them, and re-layouts, body(): ov_cols = lax.dynamic_slice_in_dim(ov_factors, offset, local_width, 2)  2.8 us
    dot_general x1, matrix products, body(): jnp.einsum('xap,pjb->xjba', dressed, ov_cols, preferred_element_type=jnp....  2.63 us
    dot_general x1, matrix products, body(): jnp.einsum('ac,pcb->pba', fock_matrix, amp_cols, preferred_element_type=j...  2.5 us
  transfers between devices with their start and end apart: 2, of which 2 were waited for; matrix products, arithmetic and copies ran while one was open for 10% of the time, Pallas kernels for 0%

commit v1 on v0

v1 whole, which is shorter than its diff:
```python
import jax
import jax.numpy as jnp
from jax import lax
from jax.experimental import pallas as pl
from jax.experimental.pallas import tpu as pltpu
from jax.sharding import PartitionSpec as P

F32, BF16 = jnp.float32, jnp.bfloat16
MESH = pl.DeviceIdType.MESH
NX, NY, NZ = 8, 8, 8
V, Q, NOCC, W = 128, 64, 64, 8
QROWS = Q // 4 * W
HALF = QROWS // 2
ORDER = (1, 7, 2, 6, 3, 5, 4)


def dot_nt(a, b):
    return lax.dot_general(a, b, (((1,), (1,)), ((), ())), preferred_element_type=F32)


def dot_nn(a, b):
    return jnp.dot(a, b, preferred_element_type=F32)


def kernel(
    amp_hbm, fac_hbm, ov_hbm, fock_hbm, screen_hbm, out_ref,
    amp, ov_raw, ov_wide, ov_by_k, fock, screen, lhs, gathered, inter, weights,
    g_near, g_pack, g_far,
    local_sem, y_send, y_recv, in_send, in_recv, sib_send, sib_recv, own_sem, g_sem,
):
    pair, virt = lax.axis_index("pair"), lax.axis_index("virt")
    x, z = pair // NZ, pair % NZ
    y, core = virt // 2, virt % 2
    color = (x + 2 * z) % 4
    sibling = (pair, y * 2 + 1 - core)

    def rows(quarter):
        return pl.ds(pl.multiple_of(quarter % 4 * QROWS, QROWS), QROWS)

    def half_rows(quarter, half):
        return pl.ds(pl.multiple_of(quarter % 4 * QROWS + half * HALF, HALF), HALF)

    def remote(src, dst, send, recv, device):
        return pltpu.make_async_remote_copy(
            src_ref=src, dst_ref=dst, send_sem=send, recv_sem=recv, device_id=device, device_id_type=MESH
        )

    loads = [
        pltpu.make_async_copy(ov_hbm, ov_raw, local_sem.at[0]),
        pltpu.make_async_copy(amp_hbm, amp, local_sem.at[1]),
        pltpu.make_async_copy(fock_hbm, fock, local_sem.at[2]),
        pltpu.make_async_copy(fac_hbm, lhs.at[pl.ds(0, Q * W)], local_sem.at[3]),
        pltpu.make_async_copy(fac_hbm, gathered.at[virt], local_sem.at[4]),
        pltpu.make_async_copy(screen_hbm, screen, local_sem.at[5]),
    ]
    for load in loads:
        load.start()

    barrier = pltpu.get_barrier_semaphore()
    peers = [(pair, (y + d) % NY * 2 + core) for d in ORDER]
    peers += [sibling]
    peers += [((x + d) % NX * NZ + z, virt) for d in range(1, NX)]
    peers += [(x * NZ + (z + d) % NZ, virt) for d in range(1, NZ)]
    for peer in peers:
        pl.semaphore_signal(barrier, inc=1, device_id=peer, device_id_type=MESH)

    loads[0].wait()
    ov_wide[...] = ov_raw[...].astype(F32)

    def split_k(k, carry):
        ov_by_k[k] = ov_wide[pl.ds(k, Q, stride=NOCC), :].astype(BF16)
        return carry

    lax.fori_loop(0, NOCC, split_k, 0, unroll=8)
    loads[1].wait()

    def dress(k, carry):
        direct, crossed = carry
        left = jnp.concatenate([ov_by_k[2 * k], ov_by_k[2 * k + 1]], axis=1)
        pair_rows = amp[pl.ds(pl.multiple_of(k * 2 * V, 2 * V), 2 * V), :]
        side = jnp.concatenate([pair_rows[:V], pair_rows[V:]], axis=1)
        return direct + dot_nt(left, side), crossed + dot_nn(left, pair_rows)

    zero = jnp.zeros((Q, V), F32)
    direct, crossed = lax.fori_loop(0, NOCC // 2, dress, (zero, zero), unroll=4)
    dressed = (2.0 * direct - crossed).astype(BF16)
    lane = lax.broadcasted_iota(jnp.int32, (16, V), 1)
    line = lax.broadcasted_iota(jnp.int32, (16, V), 0)
    chip_rows = jnp.where(lane == y * 16 + line, 1.0, 0.0).astype(BF16)
    mine = dot_nt(chip_rows, dressed)
    mine = jnp.concatenate([mine, jnp.zeros((16, V - Q), F32)], axis=1).astype(BF16)
    g_near[x] = mine

    pl.semaphore_wait(barrier, len(peers))

    sends = []

    def start(copy):
        copy.start()
        sends.append(copy)

    for d in ORDER:
        start(
            remote(
                fac_hbm.at[rows(color)], gathered.at[virt, rows(color)],
                y_send.at[d - 1], y_recv.at[d - 1], (pair, (y + d) % NY * 2 + core),
            )
        )
    start(remote(fac_hbm, gathered.at[virt], own_sem.at[0], own_sem.at[1], sibling))
    for d in range(1, NX):
        start(
            remote(
                g_near.at[x], g_near.at[x], g_sem.at[0, d - 1], g_sem.at[1, d - 1],
                ((x + d) % NX * NZ + z, virt),
            )
        )

    loads[2].wait()
    loads[3].wait()
    own_rows = jnp.where(lane == virt * W + line % W, 1.0, 0.0)
    fock_rows = dot_nt(own_rows.astype(BF16), fock[...])
    lhs[pl.ds(Q * W, 16), :] = jnp.where(line < W, fock_rows, own_rows).astype(BF16)

    def inter_step(jp, carry):
        both = dot_nt(lhs[...], amp[pl.ds(pl.multiple_of(jp * 2 * V, 2 * V), 2 * V), :])
        both = both.reshape(Q + 2, W, 2 * V)
        packed = jnp.concatenate([both[:, :, :V], both[:, :, V:]], axis=1).astype(BF16)
        inter[:, pl.ds(pl.multiple_of(jp * 16, 16), 16), :] = packed
        return carry

    def from_y(d):
        return (y - d) % NY * 2 + core

    def relay(d):
        slot, quarter = from_y(d), rows(color)
        piece = gathered.at[slot, quarter]
        remote(piece, piece, y_send.at[d - 1], y_recv.at[d - 1], sibling).wait_recv()
        start(remote(piece, piece, in_send.at[d - 1, 4], in_recv.at[d - 1, 4], sibling))
        for way, (dx, dz) in enumerate(((1, 0), (-1, 0), (0, 1), (0, -1))):
            part = piece if way < 2 else gathered.at[slot, half_rows(color, way - 2)]
            target = ((x + dx) % NX * NZ + (z + dz) % NZ, virt)
            start(remote(part, part, in_send.at[d - 1, way], in_recv.at[d - 1, way], target))

    def relay_in_plane(d):
        slot = from_y(d)
        for way, quarter in enumerate((rows(color + 3), rows(color + 1), half_rows(color + 2, 0), half_rows(color + 2, 1))):
            part = gathered.at[slot, quarter]
            remote(part, part, in_send.at[d - 1, way], in_recv.at[d - 1, way], sibling).wait_recv()
        for n in range(3):
            part = gathered.at[slot, rows(color + 1 + n)]
            start(remote(part, part, sib_send.at[d - 1, n], sib_recv.at[d - 1, n], sibling))

    steps = NOCC // 2
    for n, group in enumerate(((1, 7), (2, 6), (3, 5), (4,))):
        lax.fori_loop(steps // 4 * n, steps // 4 * (n + 1), inter_step, 0, unroll=8)
        for d in group:
            relay(d)

    for d in range(1, NX):
        there = g_near.at[(x - d) % NX]
        remote(there, there, g_sem.at[0, d - 1], g_sem.at[1, d - 1], sibling).wait_recv()

    def near_rows(n):
        wide = g_near[n].astype(F32)
        return jnp.where(core == 0, wide[:W], wide[W:])

    for m in range(NX // 2):
        low, high = near_rows(m), near_rows(m + NX // 2)
        both = jnp.concatenate([low[:, :Q], high[:, :Q]], axis=1)
        g_pack[pl.ds(m * W, W), :] = both
    g_far[z] = g_pack[...].astype(BF16)
    for d in range(1, NZ):
        start(
            remote(
                g_far.at[z], g_far.at[z], g_sem.at[2, d - 1], g_sem.at[3, d - 1],
                (x * NZ + (z + d) % NZ, virt),
            )
        )
    for d in ORDER:
        relay_in_plane(d)

    picked = []
    own_mat = own_rows.astype(BF16)
    for n in range(NOCC // 4):
        four = dot_nt(own_mat, ov_by_k[4 * n : 4 * n + 4].reshape(4 * Q, V))[:W]
        picked += [four[:, :V], four[:, V:]]
    picked = jnp.concatenate(picked, axis=0).astype(BF16)

    def twice(block):
        empty = jnp.zeros((Q, V), BF16)
        top = jnp.concatenate([block, empty], axis=1)
        return jnp.concatenate([top, jnp.concatenate([empty, block], axis=1)], axis=0)

    cycle = dot_nn(picked, twice(dressed)).reshape(NOCC // 2, W, 2 * V)
    ov_mine = ov_wide[pl.ds(pair, Q, stride=NOCC), :].astype(BF16)

    def regroup(chip):
        first = gathered[chip * 2].astype(F32).reshape(Q, W, V)
        second = gathered[chip * 2 + 1].astype(F32).reshape(Q, W, V)
        weights[:, pl.ds(pl.multiple_of(chip * 16, 16), 16), :] = jnp.concatenate([first, second], axis=1).astype(BF16)

    loads[4].wait()
    other = gathered.at[y * 2 + 1 - core]
    remote(other, other, own_sem.at[0], own_sem.at[1], sibling).wait_recv()
    regroup(y)
    for d in ORDER:
        slot = (y - d) % NY * 2 + 1 - core
        part = gathered.at[slot, rows(color)]
        remote(part, part, in_send.at[d - 1, 4], in_recv.at[d - 1, 4], sibling).wait_recv()
        for n in range(3):
            part = gathered.at[slot, rows(color + 1 + n)]
            remote(part, part, sib_send.at[d - 1, n], sib_recv.at[d - 1, n], sibling).wait_recv()
        regroup((y - d) % NY)

    total = dot_nt(inter[Q + 1], fock[...]) + inter[Q].astype(F32)
    for p in range(0, Q, 2):
        left = jnp.concatenate([inter[p], inter[p + 1]], axis=1)
        right = jnp.concatenate([weights[p], weights[p + 1]], axis=1)
        total = total + dot_nt(left, right)
    total = total.reshape(NOCC, W, V)

    for d in range(1, NZ):
        there = g_far.at[(z - d) % NZ]
        remote(there, there, g_sem.at[2, d - 1], g_sem.at[3, d - 1], sibling).wait_recv()
    mirror = dot_nn(g_far[...].reshape(NZ * NX // 2 * W, V), twice(ov_mine))
    mirror = mirror.reshape(NZ, NX // 2, W, 2 * V)

    loads[5].wait()
    for j in range(0, NOCC, 2):
        tiles = []
        for k in (j, j + 1):
            jx, jz = k // NZ, k % NZ
            lanes = slice(jx // (NX // 2) * V, (jx // (NX // 2) + 1) * V)
            tile = total[k] + cycle[k // 2, :, k % 2 * V : (k % 2 + 1) * V]
            tile = tile + mirror[jz, jx % (NX // 2), :, lanes]
            tiles.append(tile * screen[0, k].astype(F32))
        out_ref[pl.ds(j * W, 16), :] = jnp.concatenate(tiles, axis=0).astype(BF16)

    for copy in sends:
        copy.wait_send()


def body(amplitudes, factors, ov_factors, fock_matrix, screen):
    vmem, dma = pltpu.VMEM, pltpu.SemaphoreType.DMA
    out = pl.pallas_call(
        kernel,
        out_shape=jax.ShapeDtypeStruct((NOCC * W, V), BF16),
        in_specs=[pl.BlockSpec(memory_space=pl.ANY)] * 5,
        out_specs=pl.BlockSpec(memory_space=pltpu.VMEM),
        scratch_shapes=[
            vmem((NOCC * V, V), BF16),
            vmem((Q * NOCC, V), BF16),
            vmem((Q * NOCC, V), F32),
            vmem((NOCC, Q, V), BF16),
            vmem((V, V), BF16),
            pltpu.SMEM((1, NOCC), jnp.int32),
            vmem(((Q + 2) * W, V), BF16),
            vmem((NY * 2, Q * W, V), BF16),
            vmem((Q + 2, NOCC * W, V), BF16),
            vmem((Q, V, V), BF16),
            vmem((NX, 16, V), BF16),
            vmem((NX // 2 * W, V), F32),
            vmem((NZ, NX // 2 * W, V), BF16),
            dma((6,)),
            dma((NY - 1,)),
            dma((NY - 1,)),
            dma((NY - 1, 5)),
            dma((NY - 1, 5)),
            dma((NY - 1, 3)),
            dma((NY - 1, 3)),
            dma((2,)),
            dma((4, NX - 1)),
        ],
        compiler_params=pltpu.CompilerParams(
            collective_id=0, has_side_effects=True, vmem_limit_bytes=48 * 1024 * 1024
        ),
        name="residual",
    )(
        amplitudes.reshape(NOCC * V, V),
        factors.reshape(Q * W, V),
        ov_factors.reshape(Q * NOCC, V),
        fock_matrix,
        screen,
    )
    return out.reshape(NOCC, W, V)


def solution(mesh):
    in_specs = (P("pair", None, None), P(None, "virt", None), P(), P(), P("pair", None))
    out_specs = P("pair", "virt", None)
    return jax.shard_map(body, mesh=mesh, in_specs=in_specs, out_specs=out_specs, check_vma=False)
```

time: 86.6 us -> 51.1 us (0.59)
  Pallas kernels: 0 us -> 45 us
  blocking collectives: 34.5 us -> 0 us
  between operations: 13.5 us -> 0.01 us
  matrix products: 12.7 us -> 0 us
  waiting for transfers between devices: 11.5 us -> 0 us
  starting transfers between devices: 9.74 us -> 0 us
  local copies, waits for them, and re-layouts: 4.42 us -> 5.79 us
    pallas_call x0 -> x1, Pallas kernels: none -> 45 us  [body(): pl.pallas_call(kernel, out_shape=jax.ShapeDtypeStruct((NOCC * W, V), BF16...]
    all_to_all x1 -> x0, blocking collectives: 34.5 us -> none  [body(): lax.all_to_all(outgoing, 'pair', split_axis=0, concat_axis=0, tiled=True)]
    dot_general x5 -> x0, matrix products: 12.7 us -> none  [the longest x1 6.09 us: body(): jnp.einsum('qac,pqbc->pba', lax.all_gather(factors, 'virt', axis=1, tiled...]
    all_to_all x1 -> x0, starting transfers between devices: 9.73 us -> none  [body(): lax.all_to_all(lax.all_to_all(outgoing, 'pair', split_axis=0, concat_axis...]
    all_to_all x1 -> x0, waiting for transfers between devices: 7.88 us -> none  [body(): lax.all_to_all(lax.all_to_all(outgoing, 'pair', split_axis=0, concat_axis...]
    unnamed x12 -> x11, local copies, waits for them, and re-layouts: 1.13 us -> 5.79 us
    all_gather x1 -> x0, waiting for transfers between devices: 2.92 us -> none  [body(): lax.all_gather(factors, 'virt', axis=1, tiled=True)]
    dynamic_slice x1 -> x0, local copies, waits for them, and re-layouts: 2.8 us -> none  [body(): ov_cols = lax.dynamic_slice_in_dim(ov_factors, offset, local_width, 2)]
  transfers between devices with their start and end apart: 2 -> 0, of which waited for: 2 -> 0; matrix products, arithmetic and copies ran while one was open for 10% -> 0% of each run, Pallas kernels for 0% -> 0%
where the time goes in v1:
time: 51.1 us; the launch traced here: 50.8 us
  Pallas kernels  45 us (88%)
  local copies, waits for them, and re-layouts  5.79 us (11%)
    pallas_call x1, Pallas kernels, body(): pl.pallas_call(kernel, out_shape=jax.ShapeDtypeStruct((NOCC * W, V), BF16...  45 us
    unnamed x11, local copies, waits for them, and re-layouts  5.79 us

profile of v1, /device:TPU:1, one launch (start us, length us, event | category | flops | bytes accessed | tf_op | source)
XLA Modules:
  0.0 50.8 jit_solution(17400104776147053685)
XLA Ops:
  0.0 0.0 copy-start
  0.0 1.6 %copy-done = bf16[64,128,128]{2,1,0:T(8,128)(2,1)S(1)} copy-done((bf16[64,128,128]{2,1,0:T(8,128)(2,1)S(1)}, bf16[64,128,128]{2,1,0:T(8,128)(2,1)}, u32[]{:S(2)}) %copy-start) | copy-done | bytes 2097176
  1.6 0.0 copy-start.1
  1.6 1.2 %copy-done.1 = bf16[64,64,128]{2,1,0:T(8,128)(2,1)S(1)} copy-done((bf16[64,64,128]{2,1,0:T(8,128)(2,1)S(1)}, bf16[64,64,128]{2,1,0:T(8,128)(2,1)}, u32[]{:S(2)}) %copy-start.1) | copy-done | bytes 1048600
  2.8 0.0 copy-start.2
  2.8 0.9 %copy-done.2 = bf16[64,8,128]{2,1,0:T(8,128)(2,1)S(1)} copy-done((bf16[64,8,128]{2,1,0:T(8,128)(2,1)S(1)}, bf16[64,8,128]{2,1,0:T(8,128)(2,1)}, u32[]{:S(2)}) %copy-start.2) | copy-done | bytes 131096
  3.7 0.0 copy-start.3
  3.7 0.8 %copy-done.3 = bf16[128,128]{1,0:T(8,128)(2,1)S(1)} copy-done((bf16[128,128]{1,0:T(8,128)(2,1)S(1)}, bf16[128,128]{1,0:T(8,128)(2,1)}, u32[]{:S(2)}) %copy-start.3) | copy-done | bytes 32792
  4.5 0.0 copy-start.4
  4.5 0.7 %copy-done.4 = s32[1,64]{1,0:T(1,128)S(1)} copy-done((s32[1,64]{1,0:T(1,128)S(1)}, s32[1,64]{1,0:T(1,128)}, u32[]{:S(2)}) %copy-start.4) | copy-done | bytes 280
  5.1 45.0 %residual.1 = bf16[512,128]{1,0:T(8,128)(2,1)S(1)} custom-call(bf16[8192,128]{1,0:T(8,128)(2,1)S(1)} %bitcast.4, bf16[512,128]{1,0:T(8,128)(2,1)S(1)} %bitcast.7, bf16[4096,128]{1,0:T(8,128)(2,1)S(1)} %bitcast.5, bf16[128,128]{1,0:T(8,128)(2,1)S(1)} %copy-done.3, s32[1,64]{1,0:T(1,128)S(1)} %copy-done.4), custom_call_target="tpu_custom_call" | custom-call | tf_op jit(solution)/shard_map/residual/pallas_call | solution.py:245
  50.1 0.7 %copy.7 = bf16[64,8,128]{2,1,0:T(8,128)(2,1)} copy(bf16[64,8,128]{2,1,0:T(8,128)(2,1)S(1)} %bitcast.6) | data formatting | bytes 262144
Async XLA Ops:
  0.0 1.6 %copy-start = (bf16[64,128,128]{2,1,0:T(8,128)(2,1)S(1)}, bf16[64,128,128]{2,1,0:T(8,128)(2,1)}, u32[]{:S(2)}) copy-start(bf16[64,128,128]{2,1,0:T(8,128)(2,1)} %param.5) | copy-start | bytes 6291460
  1.6 1.2 %copy-start.1 = (bf16[64,64,128]{2,1,0:T(8,128)(2,1)S(1)}, bf16[64,64,128]{2,1,0:T(8,128)(2,1)}, u32[]{:S(2)}) copy-start(bf16[64,64,128]{2,1,0:T(8,128)(2,1)} %param.7) | copy-start | bytes 3145732
  2.8 0.9 %copy-start.2 = (bf16[64,8,128]{2,1,0:T(8,128)(2,1)S(1)}, bf16[64,8,128]{2,1,0:T(8,128)(2,1)}, u32[]{:S(2)}) copy-start(bf16[64,8,128]{2,1,0:T(8,128)(2,1)} %param.6) | copy-start | bytes 393220
  3.7 0.8 %copy-start.3 = (bf16[128,128]{1,0:T(8,128)(2,1)S(1)}, bf16[128,128]{1,0:T(8,128)(2,1)}, u32[]{:S(2)}) copy-start(bf16[128,128]{1,0:T(8,128)(2,1)} %fock_hbm.1) | copy-start | bytes 98308
  4.5 0.7 %copy-start.4 = (s32[1,64]{1,0:T(1,128)S(1)}, s32[1,64]{1,0:T(1,128)}, u32[]{:S(2)}) copy-start(s32[1,64]{1,0:T(1,128)} %screen_hbm.1) | copy-start | bytes 772

commit v2 on v1

--- a/solution.py
+++ b/solution.py
@@ -25,7 +25,7 @@
 def kernel(
     amp_hbm, fac_hbm, ov_hbm, fock_hbm, screen_hbm, out_ref,
     amp, ov_raw, ov_wide, ov_by_k, fock, screen, lhs, gathered, inter, weights,
-    g_near, g_pack, g_far,
+    total, g_near, g_pack, g_far,
     local_sem, y_send, y_recv, in_send, in_recv, sib_send, sib_recv, own_sem, g_sem,
 ):
     pair, virt = lax.axis_index("pair"), lax.axis_index("virt")
@@ -64,6 +64,44 @@
     for peer in peers:
         pl.semaphore_signal(barrier, inc=1, device_id=peer, device_id_type=MESH)
 
+    pl.semaphore_wait(barrier, len(peers))
+
+    sends = []
+
+    def start(copy):
+        copy.start()
+        sends.append(copy)
+
+    for d in ORDER:
+        start(
+            remote(
+                fac_hbm.at[rows(color)], gathered.at[virt, rows(color)],
+                y_send.at[d - 1], y_recv.at[d - 1], (pair, (y + d) % NY * 2 + core),
+            )
+        )
+    start(remote(fac_hbm, gathered.at[virt], own_sem.at[0], own_sem.at[1], sibling))
+    def from_y(d):
+        return (y - d) % NY * 2 + core
+
+    def relay(d):
+        slot, quarter = from_y(d), rows(color)
+        piece = gathered.at[slot, quarter]
+        remote(piece, piece, y_send.at[d - 1], y_recv.at[d - 1], sibling).wait_recv()
+        start(remote(piece, piece, in_send.at[d - 1, 4], in_recv.at[d - 1, 4], sibling))
+        for way, (dx, dz) in enumerate(((1, 0), (-1, 0), (0, 1), (0, -1))):
+            part = piece if way < 2 else gathered.at[slot, half_rows(color, way - 2)]
+            target = ((x + dx) % NX * NZ + (z + dz) % NZ, virt)
+            start(remote(part, part, in_send.at[d - 1, way], in_recv.at[d - 1, way], target))
+
+    def relay_in_plane(d):
+        slot = from_y(d)
+        for way, quarter in enumerate((rows(color + 3), rows(color + 1), half_rows(color + 2, 0), half_rows(color + 2, 1))):
+            part = gathered.at[slot, quarter]
+            remote(part, part, in_send.at[d - 1, way], in_recv.at[d - 1, way], sibling).wait_recv()
+        for n in range(3):
+            part = gathered.at[slot, rows(color + 1 + n)]
+            start(remote(part, part, sib_send.at[d - 1, n], sib_recv.at[d - 1, n], sibling))
+
     loads[0].wait()
     ov_wide[...] = ov_raw[...].astype(F32)
 
@@ -72,6 +110,8 @@
         return carry
 
     lax.fori_loop(0, NOCC, split_k, 0, unroll=8)
+    relay(1)
+    relay(7)
     loads[1].wait()
 
     def dress(k, carry):
@@ -91,22 +131,6 @@
     mine = jnp.concatenate([mine, jnp.zeros((16, V - Q), F32)], axis=1).astype(BF16)
     g_near[x] = mine
 
-    pl.semaphore_wait(barrier, len(peers))
-
-    sends = []
-
-    def start(copy):
-        copy.start()
-        sends.append(copy)
-
-    for d in ORDER:
-        start(
-            remote(
-                fac_hbm.at[rows(color)], gathered.at[virt, rows(color)],
-                y_send.at[d - 1], y_recv.at[d - 1], (pair, (y + d) % NY * 2 + core),
-            )
-        )
-    start(remote(fac_hbm, gathered.at[virt], own_sem.at[0], own_sem.at[1], sibling))
     for d in range(1, NX):
         start(
             remote(
@@ -128,33 +152,66 @@
         inter[:, pl.ds(pl.multiple_of(jp * 16, 16), 16), :] = packed
         return carry
 
-    def from_y(d):
-        return (y - d) % NY * 2 + core
-
-    def relay(d):
-        slot, quarter = from_y(d), rows(color)
-        piece = gathered.at[slot, quarter]
-        remote(piece, piece, y_send.at[d - 1], y_recv.at[d - 1], sibling).wait_recv()
-        start(remote(piece, piece, in_send.at[d - 1, 4], in_recv.at[d - 1, 4], sibling))
-        for way, (dx, dz) in enumerate(((1, 0), (-1, 0), (0, 1), (0, -1))):
-            part = piece if way < 2 else gathered.at[slot, half_rows(color, way - 2)]
-            target = ((x + dx) % NX * NZ + (z + dz) % NZ, virt)
-            start(remote(part, part, in_send.at[d - 1, way], in_recv.at[d - 1, way], target))
-
-    def relay_in_plane(d):
-        slot = from_y(d)
-        for way, quarter in enumerate((rows(color + 3), rows(color + 1), half_rows(color + 2, 0), half_rows(color + 2, 1))):
-            part = gathered.at[slot, quarter]
-            remote(part, part, in_send.at[d - 1, way], in_recv.at[d - 1, way], sibling).wait_recv()
-        for n in range(3):
-            part = gathered.at[slot, rows(color + 1 + n)]
-            start(remote(part, part, sib_send.at[d - 1, n], sib_recv.at[d - 1, n], sibling))
-
-    steps = NOCC // 2
-    for n, group in enumerate(((1, 7), (2, 6), (3, 5), (4,))):
-        lax.fori_loop(steps // 4 * n, steps // 4 * (n + 1), inter_step, 0, unroll=8)
-        for d in group:
-            relay(d)
+    part = NOCC // 8
+    lax.fori_loop(0, part, inter_step, 0, unroll=8)
+    relay(2)
+    relay(6)
+    lax.fori_loop(part, 2 * part, inter_step, 0, unroll=8)
+    relay(3)
+    relay(5)
+    relay_in_plane(1)
+    relay_in_plane(7)
+    lax.fori_loop(2 * part, 3 * part, inter_step, 0, unroll=8)
+    relay(4)
+    relay_in_plane(2)
+    relay_in_plane(6)
+    lax.fori_loop(3 * part, 4 * part, inter_step, 0, unroll=8)
+    relay_in_plane(3)
+    relay_in_plane(5)
+
+    picked = []
+    own_mat = own_rows.astype(BF16)
+    for n in range(NOCC // 4):
+        four = dot_nt(own_mat, ov_by_k[4 * n : 4 * n + 4].reshape(4 * Q, V))[:W]
+        picked += [four[:, :V], four[:, V:]]
+    picked = jnp.concatenate(picked, axis=0).astype(BF16)
+
+    def twice(block):
+        empty = jnp.zeros((Q, V), BF16)
+        top = jnp.concatenate([block, empty], axis=1)
+        return jnp.concatenate([top, jnp.concatenate([empty, block], axis=1)], axis=0)
+
+    cycle = dot_nn(picked, twice(dressed)).reshape(NOCC // 2, W, 2 * V)
+    ov_mine = ov_wide[pl.ds(pair, Q, stride=NOCC), :].astype(BF16)
+
+    relay_in_plane(4)
+
+    def ladder(quarter):
+        span = rows(quarter)
+        first = pl.multiple_of(quarter % 4 * (Q // 4), Q // 4)
+        for chip in range(NY):
+            one = gathered[2 * chip, span, :].astype(F32).reshape(Q // 4, W, V)
+            two = gathered[2 * chip + 1, span, :].astype(F32).reshape(Q // 4, W, V)
+            weights[pl.ds(first, Q // 4), chip * 16 : chip * 16 + 16, :] = jnp.concatenate([one, two], axis=1).astype(BF16)
+        for m in range(0, NOCC * W, 256):
+            block = None
+            for p in range(0, Q // 4, 2):
+                left = [inter[first + p + n, m : m + 256] for n in range(2)]
+                right = [weights[first + p + n] for n in range(2)]
+                term = dot_nt(jnp.concatenate(left, axis=1), jnp.concatenate(right, axis=1))
+                block = term if block is None else block + term
+            total[m : m + 256] += block
+
+    for m in range(0, NOCC * W, 256):
+        block = dot_nt(inter[Q + 1, m : m + 256], fock[...])
+        total[m : m + 256] = block + inter[Q, m : m + 256].astype(F32)
+    loads[4].wait()
+    other = gathered.at[y * 2 + 1 - core]
+    remote(other, other, own_sem.at[0], own_sem.at[1], sibling).wait_recv()
+    for d in ORDER:
+        there = gathered.at[(y - d) % NY * 2 + 1 - core, rows(color)]
+        remote(there, there, in_send.at[d - 1, 4], in_recv.at[d - 1, 4], sibling).wait_recv()
+    ladder(color)
 
     for d in range(1, NX):
         there = g_near.at[(x - d) % NX]
@@ -176,48 +233,11 @@
                 (x * NZ + (z + d) % NZ, virt),
             )
         )
-    for d in ORDER:
-        relay_in_plane(d)
-
-    picked = []
-    own_mat = own_rows.astype(BF16)
-    for n in range(NOCC // 4):
-        four = dot_nt(own_mat, ov_by_k[4 * n : 4 * n + 4].reshape(4 * Q, V))[:W]
-        picked += [four[:, :V], four[:, V:]]
-    picked = jnp.concatenate(picked, axis=0).astype(BF16)
-
-    def twice(block):
-        empty = jnp.zeros((Q, V), BF16)
-        top = jnp.concatenate([block, empty], axis=1)
-        return jnp.concatenate([top, jnp.concatenate([empty, block], axis=1)], axis=0)
-
-    cycle = dot_nn(picked, twice(dressed)).reshape(NOCC // 2, W, 2 * V)
-    ov_mine = ov_wide[pl.ds(pair, Q, stride=NOCC), :].astype(BF16)
-
-    def regroup(chip):
-        first = gathered[chip * 2].astype(F32).reshape(Q, W, V)
-        second = gathered[chip * 2 + 1].astype(F32).reshape(Q, W, V)
-        weights[:, pl.ds(pl.multiple_of(chip * 16, 16), 16), :] = jnp.concatenate([first, second], axis=1).astype(BF16)
-
-    loads[4].wait()
-    other = gathered.at[y * 2 + 1 - core]
-    remote(other, other, own_sem.at[0], own_sem.at[1], sibling).wait_recv()
-    regroup(y)
-    for d in ORDER:
-        slot = (y - d) % NY * 2 + 1 - core
-        part = gathered.at[slot, rows(color)]
-        remote(part, part, in_send.at[d - 1, 4], in_recv.at[d - 1, 4], sibling).wait_recv()
-        for n in range(3):
-            part = gathered.at[slot, rows(color + 1 + n)]
-            remote(part, part, sib_send.at[d - 1, n], sib_recv.at[d - 1, n], sibling).wait_recv()
-        regroup((y - d) % NY)
-
-    total = dot_nt(inter[Q + 1], fock[...]) + inter[Q].astype(F32)
-    for p in range(0, Q, 2):
-        left = jnp.concatenate([inter[p], inter[p + 1]], axis=1)
-        right = jnp.concatenate([weights[p], weights[p + 1]], axis=1)
-        total = total + dot_nt(left, right)
-    total = total.reshape(NOCC, W, V)
+    for n in (1, 0, 2):
+        for d in ORDER:
+            there = gathered.at[(y - d) % NY * 2 + 1 - core, rows(color + 1 + n)]
+            remote(there, there, sib_send.at[d - 1, n], sib_recv.at[d - 1, n], sibling).wait_recv()
+        ladder(color + 1 + n)
 
     for d in range(1, NZ):
         there = g_far.at[(z - d) % NZ]
@@ -231,7 +251,7 @@
         for k in (j, j + 1):
             jx, jz = k // NZ, k % NZ
             lanes = slice(jx // (NX // 2) * V, (jx // (NX // 2) + 1) * V)
-            tile = total[k] + cycle[k // 2, :, k % 2 * V : (k % 2 + 1) * V]
+            tile = total[k * W : (k + 1) * W] + cycle[k // 2, :, k % 2 * V : (k % 2 + 1) * V]
             tile = tile + mirror[jz, jx % (NX // 2), :, lanes]
             tiles.append(tile * screen[0, k].astype(F32))
         out_ref[pl.ds(j * W, 16), :] = jnp.concatenate(tiles, axis=0).astype(BF16)
@@ -258,6 +278,7 @@
             vmem((NY * 2, Q * W, V), BF16),
             vmem((Q + 2, NOCC * W, V), BF16),
             vmem((Q, V, V), BF16),
+            vmem((NOCC * W, V), F32),
             vmem((NX, 16, V), BF16),
             vmem((NX // 2 * W, V), F32),
             vmem((NZ, NX // 2 * W, V), BF16),
@@ -272,7 +293,7 @@
             dma((4, NX - 1)),
         ],
         compiler_params=pltpu.CompilerParams(
-            collective_id=0, has_side_effects=True, vmem_limit_bytes=48 * 1024 * 1024
+            collective_id=0, has_side_effects=True, vmem_limit_bytes=62 * 1024 * 1024
         ),
         name="residual",
     )(

time: 51.1 us -> 44.7 us (0.87)
  local copies, waits for them, and re-layouts: 5.79 us -> 1.57 us
  Pallas kernels: 45 us -> 42.9 us
    unnamed x11 -> x1, local copies, waits for them, and re-layouts: 5.79 us -> 1.57 us
    pallas_call x1, Pallas kernels: 45 us -> 42.9 us  [body(): pl.pallas_call(kernel, out_shape=jax.ShapeDtypeStruct((NOCC * W, V), BF16...]
where the time goes in v2:
time: 44.7 us; the launch traced here: 44.5 us
  Pallas kernels  42.9 us (96%)
  local copies, waits for them, and re-layouts  1.57 us (4%)
    pallas_call x1, Pallas kernels, body(): pl.pallas_call(kernel, out_shape=jax.ShapeDtypeStruct((NOCC * W, V), BF16...  42.9 us
    unnamed x1, local copies, waits for them, and re-layouts  1.57 us

profile of v2, /device:TPU:1, one launch (start us, length us, event | category | flops | bytes accessed | tf_op | source)
XLA Modules:
  0.0 44.5 jit_solution(10057285283491063701)
XLA Ops:
  0.0 42.9 %residual.1 = bf16[512,128]{1,0:T(8,128)(2,1)} custom-call(bf16[8192,128]{1,0:T(8,128)(2,1)} %bitcast.4, bf16[512,128]{1,0:T(8,128)(2,1)} %bitcast.7, bf16[4096,128]{1,0:T(8,128)(2,1)} %bitcast.5, bf16[128,128]{1,0:T(8,128)(2,1)} %fock_hbm.1, s32[1,64]{1,0:T(1,128)} %screen_hbm.1), custom_call_target="tpu_custom_call" | custom-call | tf_op jit(solution)/shard_map/residual/pallas_call | solution.py:265
  42.9 1.6 %copy.7 = bf16[64,8,128]{2,1,0:T(8,128)(2,1)} copy(bf16[64,8,128]{2,1,0:T(8,128)(2,1)} %bitcast.6) | data formatting | bytes 262144

commit v3 on v2

v3 whole, which is shorter than its diff:
```python
import functools

import jax
import jax.numpy as jnp
from jax import lax
from jax.experimental import pallas as pl
from jax.experimental.pallas import tpu as pltpu
from jax.sharding import PartitionSpec as P

F32, BF16 = jnp.float32, jnp.bfloat16
MESH = pl.DeviceIdType.MESH
NX, NY, NZ = 8, 8, 8
V, Q, NOCC, W = 128, 64, 64, 8
QROWS = Q // 4 * W
PARTS = 4
ORDER = (1, 7, 2, 6, 3, 5, 4)


def dot_nt(a, b):
    return lax.dot_general(a, b, (((1,), (1,)), ((), ())), preferred_element_type=F32)


def dot_nn(a, b):
    return jnp.dot(a, b, preferred_element_type=F32)


def kernel(
    amp_hbm, fac_hbm, ov_hbm, fock_hbm, screen_hbm, out_ref,
    amp, ov_raw, ov_wide, ov_by_k, fock, screen, lhs, gathered, inter, weights,
    total, g_near, g_pack, g_far,
    local_sem, amp_sem, y_send, y_recv, in_send, in_recv, sib_send, sib_recv, own_sem, g_sem, ready,
):
    pair, virt = lax.axis_index("pair"), lax.axis_index("virt")
    x, z = pair // NZ, pair % NZ
    y, core = virt // 2, virt % 2
    color = (x + 2 * z) % 4
    sibling = (pair, y * 2 + 1 - core)

    def rows(quarter):
        return pl.ds(pl.multiple_of(quarter % 4 * QROWS, QROWS), QROWS)

    def remote(src, dst, send, recv, device):
        return pltpu.make_async_remote_copy(
            src_ref=src, dst_ref=dst, send_sem=send, recv_sem=recv, device_id=device, device_id_type=MESH
        )

    def amp_load(n):
        span = pl.ds(n * NOCC * V // PARTS, NOCC * V // PARTS)
        return pltpu.make_async_copy(amp_hbm.at[span], amp.at[span], amp_sem.at[n])

    ov_load = pltpu.make_async_copy(ov_hbm, ov_raw, local_sem.at[0])
    ov_load.start()
    for n in range(PARTS):
        amp_load(n).start()
    loads = [
        pltpu.make_async_copy(fock_hbm, fock, local_sem.at[2]),
        pltpu.make_async_copy(fac_hbm, lhs.at[pl.ds(0, Q * W)], local_sem.at[3]),
        pltpu.make_async_copy(fac_hbm, gathered.at[virt], local_sem.at[4]),
        pltpu.make_async_copy(screen_hbm, screen, local_sem.at[5]),
    ]
    for load in loads:
        load.start()

    def key(px, py, pz, pc):
        hops = jnp.minimum(px, NX - px) + jnp.minimum(py, NY - py)
        number = ((px * NZ + pz) * NY + py) * 2 + pc
        return jnp.where(number == 0, 9 * NZ // 2 * 1024 - 1, (pz * 9 + hops) * 1024 + number)

    mine = key(x, y, z, core)
    peers, answers, later = [], [], []
    for axis in range(3):
        for d in range(1, 8):
            at = [x, y, z]
            at[axis] = (at[axis] + d) % 8
            peers.append((at[0] * NZ + at[2], at[1] * 2 + core))
            answers.append(axis * 7 + 7 - d)
            later.append(key(*at, core) > mine)
    peers.append(sibling)
    answers.append(21)
    later.append(key(x, y, z, 1 - core) > mine)

    def signal(semaphore, device):
        pl.semaphore_signal(semaphore, inc=1, device_id=device, device_id_type=MESH)

    barrier = pltpu.get_barrier_semaphore()
    for peer, is_later in zip(peers, later):
        pl.when(is_later)(functools.partial(signal, barrier, peer))
    earlier_count = sum(jnp.where(is_later, 0, 1) for is_later in later)

    def ensure(slot):
        pl.when(later[slot])(functools.partial(pl.semaphore_wait, ready.at[slot], 1))

    def slot_of(axis, d):
        return axis * 7 + d - 1

    sends = []

    def start(copy):
        copy.start()
        sends.append((None, copy))

    def start_if(condition, copy):
        pl.when(condition)(copy.start)
        sends.append((condition, copy))

    def from_y(d):
        return (y - d) % NY * 2 + core

    def relay(d):
        slot, quarter = from_y(d), rows(color)
        piece = gathered.at[slot, quarter]
        remote(piece, piece, y_send.at[d - 1], y_recv.at[d - 1], sibling).wait_recv()
        start(remote(piece, piece, in_send.at[d - 1, 3], in_recv.at[d - 1, 3], sibling))
        for way, target in enumerate(((x + 1) % NX * NZ + z, (x + NX - 1) % NX * NZ + z, x * NZ + z + 1 - z % 2 * 2)):
            start(remote(piece, piece, in_send.at[d - 1, way], in_recv.at[d - 1, way], (target, virt)))

    def relay_in_plane(d):
        slot = from_y(d)
        for way, quarter in enumerate((rows(color + 3), rows(color + 1), rows(color + 2))):
            part = gathered.at[slot, quarter]
            remote(part, part, in_send.at[d - 1, way], in_recv.at[d - 1, way], sibling).wait_recv()
        for n in range(3):
            part = gathered.at[slot, rows(color + 1 + n)]
            start(remote(part, part, sib_send.at[d - 1, n], sib_recv.at[d - 1, n], sibling))

    ov_load.wait()
    ov_wide[...] = ov_raw[...].astype(F32)

    def split_k(k, carry):
        ov_by_k[k] = ov_wide[pl.ds(k, Q, stride=NOCC), :].astype(BF16)
        return carry

    lax.fori_loop(0, NOCC, split_k, 0, unroll=8)

    pl.when(earlier_count > 0)(functools.partial(pl.semaphore_wait, barrier, earlier_count))
    for slot in range(22):
        pl.when(jnp.logical_not(later[slot]))(functools.partial(signal, ready.at[answers[slot]], peers[slot]))

    def y_copy(d):
        return remote(
            fac_hbm.at[rows(color)], gathered.at[virt, rows(color)], y_send.at[d - 1], y_recv.at[d - 1], peers[slot_of(1, d)]
        )

    def z_copy(d):
        return remote(g_near.at[z], g_near.at[z], g_sem.at[0, d - 1], g_sem.at[1, d - 1], peers[slot_of(2, d)])

    def send_earlier(slot, copy):
        start_if(jnp.logical_not(later[slot]), copy)

    def send_later(slot, copy):
        ensure(slot)
        start_if(later[slot], copy)

    for d in ORDER:
        send_earlier(slot_of(1, d), y_copy(d))

    def dress(k, carry):
        direct, crossed = carry
        left = jnp.concatenate([ov_by_k[2 * k], ov_by_k[2 * k + 1]], axis=1)
        pair_rows = amp[pl.ds(pl.multiple_of(k * 2 * V, 2 * V), 2 * V), :]
        side = jnp.concatenate([pair_rows[:V], pair_rows[V:]], axis=1)
        return direct + dot_nt(left, side), crossed + dot_nn(left, pair_rows)

    zero = jnp.zeros((Q, V), F32)
    sums = (zero, zero)
    for n in range(PARTS):
        amp_load(n).wait()
        share = NOCC // 2 // PARTS
        sums = lax.fori_loop(n * share, (n + 1) * share, dress, sums, unroll=4)
    direct, crossed = sums
    dressed = (2.0 * direct - crossed).astype(BF16)
    lane = lax.broadcasted_iota(jnp.int32, (16, V), 1)
    line = lax.broadcasted_iota(jnp.int32, (16, V), 0)
    chip_rows = jnp.where(lane == y * 16 + line, 1.0, 0.0).astype(BF16)
    rows_out = dot_nt(chip_rows, dressed)
    rows_out = jnp.concatenate([rows_out, jnp.zeros((16, V - Q), F32)], axis=1).astype(BF16)
    g_near[z] = rows_out
    for d in ORDER:
        send_earlier(slot_of(2, d), z_copy(d))

    loads[0].wait()
    loads[1].wait()
    own_rows = jnp.where(lane == virt * W + line % W, 1.0, 0.0)
    fock_rows = dot_nt(own_rows.astype(BF16), fock[...])
    lhs[pl.ds(Q * W, 16), :] = jnp.where(line < W, fock_rows, own_rows).astype(BF16)

    def inter_step(jp, carry):
        both = dot_nt(lhs[...], amp[pl.ds(pl.multiple_of(jp * 2 * V, 2 * V), 2 * V), :])
        both = both.reshape(Q + 2, W, 2 * V)
        packed = jnp.concatenate([both[:, :, :V], both[:, :, V:]], axis=1).astype(BF16)
        inter[:, pl.ds(pl.multiple_of(jp * 16, 16), 16), :] = packed
        return carry

    part = NOCC // 8
    for n, group in enumerate(((1, 7), (2, 6), (3, 5), (4,))):
        lax.fori_loop(n * part, (n + 1) * part, inter_step, 0, unroll=8)
        for d in group:
            send_later(slot_of(1, d), y_copy(d))
    ensure(21)
    start(remote(fac_hbm, gathered.at[virt], own_sem.at[0], own_sem.at[1], sibling))
    even = z % 2 == 0
    ensure(slot_of(0, 1))
    ensure(slot_of(0, 7))
    pl.when(even)(functools.partial(ensure, slot_of(2, 1)))
    pl.when(jnp.logical_not(even))(functools.partial(ensure, slot_of(2, 7)))
    for d in ORDER:
        relay(d)

    pl.when(jnp.logical_not(even))(functools.partial(ensure, slot_of(2, 1)))
    pl.when(even)(functools.partial(ensure, slot_of(2, 7)))
    for d in range(1, NZ):
        if d not in (1, 7):
            ensure(slot_of(2, d))
        start_if(later[slot_of(2, d)], z_copy(d))

    for d in range(1, NZ):
        there = g_near.at[(z - d) % NZ]
        remote(there, there, g_sem.at[0, d - 1], g_sem.at[1, d - 1], sibling).wait_recv()

    def near_rows(n):
        wide = g_near[n].astype(F32)
        return jnp.where(core == 0, wide[:W], wide[W:])

    for m in range(NZ // 2):
        low, high = near_rows(m), near_rows(m + NZ // 2)
        both = jnp.concatenate([low[:, :Q], high[:, :Q]], axis=1)
        g_pack[pl.ds(m * W, W), :] = both
    g_far[x] = g_pack[...].astype(BF16)
    for d in range(2, NX - 1):
        ensure(slot_of(0, d))
    for d in range(1, NX):
        start(remote(g_far.at[x], g_far.at[x], g_sem.at[2, d - 1], g_sem.at[3, d - 1], peers[slot_of(0, d)]))
    for d in ORDER:
        relay_in_plane(d)

    picked = []
    own_mat = own_rows.astype(BF16)
    for n in range(NOCC // 4):
        four = dot_nt(own_mat, ov_by_k[4 * n : 4 * n + 4].reshape(4 * Q, V))[:W]
        picked += [four[:, :V], four[:, V:]]
    picked = jnp.concatenate(picked, axis=0).astype(BF16)

    def twice(block):
        empty = jnp.zeros((Q, V), BF16)
        top = jnp.concatenate([block, empty], axis=1)
        return jnp.concatenate([top, jnp.concatenate([empty, block], axis=1)], axis=0)

    cycle = dot_nn(picked, twice(dressed)).reshape(NOCC // 2, W, 2 * V)
    cycle = jnp.concatenate([cycle[:, :, :V], cycle[:, :, V:]], axis=1).reshape(NOCC * W, V)
    ov_mine = ov_wide[pl.ds(pair, Q, stride=NOCC), :].astype(BF16)

    def ladder(quarter):
        span = rows(quarter)
        first = pl.multiple_of(quarter % 4 * (Q // 4), Q // 4)
        for chip in range(NY):
            one = gathered[2 * chip, span, :].astype(F32).reshape(Q // 4, W, V)
            two = gathered[2 * chip + 1, span, :].astype(F32).reshape(Q // 4, W, V)
            weights[pl.ds(first, Q // 4), chip * 16 : chip * 16 + 16, :] = jnp.concatenate([one, two], axis=1).astype(BF16)
        for m in range(0, NOCC * W, 256):
            block = None
            for p in range(0, Q // 4, 2):
                left = [inter[first + p + n, m : m + 256] for n in range(2)]
                right = [weights[first + p + n] for n in range(2)]
                term = dot_nt(jnp.concatenate(left, axis=1), jnp.concatenate(right, axis=1))
                block = term if block is None else block + term
            total[m : m + 256] += block

    for m in range(0, NOCC * W, 256):
        block = dot_nt(inter[Q + 1, m : m + 256], fock[...])
        total[m : m + 256] = block + inter[Q, m : m + 256].astype(F32) + cycle[m : m + 256]
    loads[2].wait()
    other = gathered.at[y * 2 + 1 - core]
    remote(other, other, own_sem.at[0], own_sem.at[1], sibling).wait_recv()
    for d in ORDER:
        there = gathered.at[(y - d) % NY * 2 + 1 - core, rows(color)]
        remote(there, there, in_send.at[d - 1, 3], in_recv.at[d - 1, 3], sibling).wait_recv()
    ladder(color)

    for n in (1, 0, 2):
        for d in ORDER:
            there = gathered.at[(y - d) % NY * 2 + 1 - core, rows(color + 1 + n)]
            remote(there, there, sib_send.at[d - 1, n], sib_recv.at[d - 1, n], sibling).wait_recv()
        ladder(color + 1 + n)

    for d in range(1, NX):
        there = g_far.at[(x - d) % NX]
        remote(there, there, g_sem.at[2, d - 1], g_sem.at[3, d - 1], sibling).wait_recv()
    mirror = dot_nn(g_far[...].reshape(NX * NZ // 2 * W, V), twice(ov_mine))
    mirror = mirror.reshape(NX, NZ // 2, W, 2 * V)

    loads[3].wait()
    for j in range(0, NOCC, 2):
        tiles = []
        for k in (j, j + 1):
            jx, jz = k // NZ, k % NZ
            lanes = slice(jz // (NZ // 2) * V, (jz // (NZ // 2) + 1) * V)
            tile = total[k * W : (k + 1) * W] + mirror[jx, jz % (NZ // 2), :, lanes]
            tiles.append(tile * screen[0, k].astype(F32))
        out_ref[pl.ds(j * W, 16), :] = jnp.concatenate(tiles, axis=0).astype(BF16)

    for condition, copy in sends:
        if condition is None:
            copy.wait_send()
        else:
            pl.when(condition)(copy.wait_send)


def body(amplitudes, factors, ov_factors, fock_matrix, screen):
    vmem, dma = pltpu.VMEM, pltpu.SemaphoreType.DMA
    out = pl.pallas_call(
        kernel,
        out_shape=jax.ShapeDtypeStruct((NOCC * W, V), BF16),
        in_specs=[pl.BlockSpec(memory_space=pl.ANY)] * 5,
        out_specs=pl.BlockSpec(memory_space=pltpu.VMEM),
        scratch_shapes=[
            vmem((NOCC * V, V), BF16),
            vmem((Q * NOCC, V), BF16),
            vmem((Q * NOCC, V), F32),
            vmem((NOCC, Q, V), BF16),
            vmem((V, V), BF16),
            pltpu.SMEM((1, NOCC), jnp.int32),
            vmem(((Q + 2) * W, V), BF16),
            vmem((NY * 2, Q * W, V), BF16),
            vmem((Q + 2, NOCC * W, V), BF16),
            vmem((Q, V, V), BF16),
            vmem((NOCC * W, V), F32),
            vmem((NX, 16, V), BF16),
            vmem((NX // 2 * W, V), F32),
            vmem((NX, NZ // 2 * W, V), BF16),
            dma((6,)),
            dma((PARTS,)),
            dma((NY - 1,)),
            dma((NY - 1,)),
            dma((NY - 1, 4)),
            dma((NY - 1, 4)),
            dma((NY - 1, 3)),
            dma((NY - 1, 3)),
            dma((2,)),
            dma((4, NX - 1)),
            pltpu.SemaphoreType.REGULAR((22,)),
        ],
        compiler_params=pltpu.CompilerParams(
            collective_id=0, has_side_effects=True, vmem_limit_bytes=62 * 1024 * 1024
        ),
        name="residual",
    )(
        amplitudes.reshape(NOCC * V, V),
        factors.reshape(Q * W, V),
        ov_factors.reshape(Q * NOCC, V),
        fock_matrix,
        screen,
    )
    return out.reshape(NOCC, W, V)


def solution(mesh):
    in_specs = (P("pair", None, None), P(None, "virt", None), P(), P(), P("pair", None))
    out_specs = P("pair", "virt", None)
    return jax.shard_map(body, mesh=mesh, in_specs=in_specs, out_specs=out_specs, check_vma=False)
```

time: 44.7 us -> 36.1 us (0.81)
  Pallas kernels: 42.9 us -> 34.2 us
    pallas_call x1, Pallas kernels: 42.9 us -> 34.2 us  [body(): pl.pallas_call(kernel, out_shape=jax.ShapeDtypeStruct((NOCC * W, V), BF16...]
where the time goes in v3:
time: 36.1 us; the launch traced here: 35.8 us
  Pallas kernels  34.2 us (95%)
  local copies, waits for them, and re-layouts  1.57 us (4%)
    pallas_call x1, Pallas kernels, body(): pl.pallas_call(kernel, out_shape=jax.ShapeDtypeStruct((NOCC * W, V), BF16...  34.2 us
    unnamed x1, local copies, waits for them, and re-layouts  1.57 us

profile of v3, /device:TPU:1, one launch (start us, length us, event | category | flops | bytes accessed | tf_op | source)
XLA Modules:
  0.0 35.8 jit_solution(321290659202765490)
XLA Ops:
  0.0 34.2 %residual.1 = bf16[512,128]{1,0:T(8,128)(2,1)} custom-call(bf16[8192,128]{1,0:T(8,128)(2,1)} %bitcast.4, bf16[512,128]{1,0:T(8,128)(2,1)} %bitcast.7, bf16[4096,128]{1,0:T(8,128)(2,1)} %bitcast.5, bf16[128,128]{1,0:T(8,128)(2,1)} %fock_hbm.1, s32[1,64]{1,0:T(1,128)} %screen_hbm.1), custom_call_target="tpu_custom_call" | custom-call | tf_op jit(solution)/shard_map/residual/pallas_call | solution.py:310
  34.2 1.6 %copy.7 = bf16[64,8,128]{2,1,0:T(8,128)(2,1)} copy(bf16[64,8,128]{2,1,0:T(8,128)(2,1)} %bitcast.6) | data formatting | bytes 262144

commit v4 on v3

v4 whole, which is shorter than its diff:
```python
import functools

import jax
import jax.numpy as jnp
from jax import lax
from jax.experimental import pallas as pl
from jax.experimental.pallas import tpu as pltpu
from jax.sharding import PartitionSpec as P

F32, BF16 = jnp.float32, jnp.bfloat16
MESH = pl.DeviceIdType.MESH
NX, NY, NZ = 8, 8, 8
V, Q, NOCC, W = 128, 64, 64, 8
QROWS = Q // 4 * W
PARTS = 4
ORDER = (1, 7, 2, 6, 3, 5, 4)
GROUPS = ((0, 4), (4, 7))


def dot_nt(a, b):
    return lax.dot_general(a, b, (((1,), (1,)), ((), ())), preferred_element_type=F32)


def dot_nn(a, b):
    return jnp.dot(a, b, preferred_element_type=F32)


def kernel(
    amp_hbm, fac_hbm, ov_hbm, fock_hbm, screen_hbm, out_ref,
    amp, ov_raw, ov_wide, ov_by_k, fock, screen, lhs, gathered, inter, weights,
    total, g_parts, g_near, g_pack, g_far,
    local_sem, ov_sem, amp_sem, part_sem, y_send, y_recv, in_send, in_recv, sib_send, sib_recv, own_sem, g_sem, ready,
):
    pair, virt = lax.axis_index("pair"), lax.axis_index("virt")
    x, z = pair // NZ, pair % NZ
    y, core = virt // 2, virt % 2
    color = (x + 2 * z) % 4
    sibling = (pair, y * 2 + 1 - core)

    def remote(src, dst, send, recv, device):
        return pltpu.make_async_remote_copy(
            src_ref=src, dst_ref=dst, send_sem=send, recv_sem=recv, device_id=device, device_id_type=MESH
        )

    def amp_load(n):
        number = (core * (PARTS // 2) + n) % PARTS
        span = pl.ds(pl.multiple_of(number * (NOCC * V // PARTS), NOCC * V // PARTS), NOCC * V // PARTS)
        return pltpu.make_async_copy(amp_hbm.at[span], amp.at[span], amp_sem.at[n])

    def ov_load(half):
        span = pl.ds(pl.multiple_of(half * (NOCC // 2), NOCC // 2), NOCC // 2)
        return pltpu.make_async_copy(ov_hbm.at[:, span], ov_raw.at[:, span], ov_sem.at[half])

    ov_load(core).start()
    for n in range(PARTS // 2):
        amp_load(n).start()
    ov_load(1 - core).start()
    for n in range(PARTS // 2, PARTS):
        amp_load(n).start()
    loads = [
        pltpu.make_async_copy(fock_hbm, fock, local_sem.at[2]),
        pltpu.make_async_copy(fac_hbm, gathered.at[:, core, NY - 1], local_sem.at[3]),
        pltpu.make_async_copy(screen_hbm, screen, local_sem.at[5]),
    ]
    for load in loads:
        load.start()

    def key(px, py, pz, pc):
        hops = jnp.minimum(px, NX - px) + jnp.minimum(py, NY - py)
        number = ((px * NZ + pz) * NY + py) * 2 + pc
        return jnp.where(number == 0, 9 * NZ // 2 * 1024 - 1, (pz * 9 + hops) * 1024 + number)

    mine = key(x, y, z, core)
    peers, answers, later = [], [], []
    for axis in range(3):
        for d in range(1, 8):
            at = [x, y, z]
            at[axis] = (at[axis] + d) % 8
            peers.append((at[0] * NZ + at[2], at[1] * 2 + core))
            answers.append(axis * 7 + 7 - d)
            later.append(key(*at, core) > mine)
    peers.append(sibling)
    answers.append(21)
    later.append(key(x, y, z, 1 - core) > mine)

    def signal(semaphore, device):
        pl.semaphore_signal(semaphore, inc=1, device_id=device, device_id_type=MESH)

    barrier = pltpu.get_barrier_semaphore()
    for peer, is_later in zip(peers, later):
        pl.when(is_later)(functools.partial(signal, barrier, peer))
    earlier_count = sum(jnp.where(is_later, 0, 1) for is_later in later)

    def ensure(slot):
        pl.when(later[slot])(functools.partial(pl.semaphore_wait, ready.at[slot], 1))

    def slot_of(axis, d):
        return axis * 7 + d - 1

    sends = []

    def start(copy):
        copy.start()
        sends.append((None, copy))

    def start_if(condition, copy):
        pl.when(condition)(copy.start)
        sends.append((condition, copy))

    def drain():
        for condition, copy in sends:
            if condition is None:
                copy.wait_send()
            else:
                pl.when(condition)(copy.wait_send)
        sends.clear()

    def block(quarter, which_core, group):
        return gathered.at[quarter % 4, which_core, pl.ds(group[0], group[1] - group[0])]

    def relay(g):
        group = GROUPS[g]
        for place in range(*group):
            there = gathered.at[color, core, place]
            remote(there, there, y_send.at[place], y_recv.at[place], sibling).wait_recv()
        piece = block(color, core, group)
        targets = ((x + 1) % NX * NZ + z, (x + NX - 1) % NX * NZ + z, x * NZ + z + 1 - z % 2 * 2)
        for way, target in enumerate(targets):
            start(remote(piece, piece, in_send.at[g, way], in_recv.at[g, way], (target, virt)))
        start(remote(piece, piece, in_send.at[g, 3], in_recv.at[g, 3], sibling))

    def relay_in_plane(copies):
        for n, way in ((1, 2), (0, 1), (2, 0)):
            for g in range(2):
                piece = block(color + 1 + n, core, GROUPS[g])
                remote(piece, piece, in_send.at[g, way], in_recv.at[g, way], sibling).wait_recv()
                copies.append(remote(piece, piece, sib_send.at[g, n], sib_recv.at[g, n], sibling))
                copies[-1].start()

    def y_copy(d):
        place = ORDER.index(d)
        there = gathered.at[color, core, place]
        return remote(fac_hbm.at[color], there, y_send.at[place], y_recv.at[place], peers[slot_of(1, d)])

    def z_copy(d):
        return remote(g_near.at[z], g_near.at[z], g_sem.at[0, d - 1], g_sem.at[1, d - 1], peers[slot_of(2, d)])

    def send_earlier(slot, copy):
        start_if(jnp.logical_not(later[slot]), copy)

    def send_later(slot, copy):
        ensure(slot)
        start_if(later[slot], copy)

    def answer(slot):
        signal(ready.at[answers[slot]], peers[slot])

    def enter():
        pl.when(earlier_count > 0)(functools.partial(pl.semaphore_wait, barrier, earlier_count))
        for slot in range(21, -1, -1):
            pl.when(jnp.logical_not(later[slot]))(functools.partial(answer, slot))
        for d in ORDER:
            pl.when(jnp.logical_not(later[slot_of(1, d)]))(y_copy(d).start)

    leading = (pair == 0) & (y == 0)
    pl.when(leading)(enter)

    def split(half):
        ov_load(half).wait()
        first = half * (NOCC // 2)
        raw = ov_raw[:, pl.ds(pl.multiple_of(first, NOCC // 2), NOCC // 2), :]
        span = pl.ds(pl.multiple_of(first * Q, NOCC // 2 * Q), NOCC // 2 * Q)
        ov_wide[span, :] = raw.astype(F32).reshape(NOCC // 2 * Q, V)

        def split_k(k, carry):
            ov_by_k[first + k] = ov_wide[pl.ds(first * Q + k, Q, stride=NOCC // 2), :].astype(BF16)
            return carry

        lax.fori_loop(0, NOCC // 2, split_k, 0, unroll=8)

    split(core)

    def dress(first, n, carry):
        k = first + n
        direct, crossed = carry
        left = jnp.concatenate([ov_by_k[2 * k], ov_by_k[2 * k + 1]], axis=1)
        pair_rows = amp[pl.ds(pl.multiple_of(k * 2 * V, 2 * V), 2 * V), :]
        side = jnp.concatenate([pair_rows[:V], pair_rows[V:]], axis=1)
        return direct + dot_nt(left, side), crossed + dot_nn(left, pair_rows)

    zero = jnp.zeros((Q, V), F32)
    sums = (zero, zero)
    share = NOCC // 2 // PARTS
    for n in range(PARTS // 2):
        amp_load(n).wait()
        first = core * (NOCC // 4) + n * share
        sums = lax.fori_loop(0, share, functools.partial(dress, first), sums, unroll=4)
    g_parts[0] = 2.0 * sums[0] - sums[1]

    pl.when(jnp.logical_not(leading))(enter)
    sends.extend((jnp.logical_not(later[slot_of(1, d)]), y_copy(d)) for d in ORDER)
    ensure(21)
    part_copy = remote(g_parts.at[0], g_parts.at[1], part_sem.at[0], part_sem.at[1], sibling)
    start(part_copy)
    start(remote(fac_hbm, gathered.at[:, core, NY - 1], own_sem.at[0], own_sem.at[1], sibling))
    part_copy.wait_recv()
    dressed = (g_parts[0] + g_parts[1]).astype(BF16)
    lane = lax.broadcasted_iota(jnp.int32, (16, V), 1)
    line = lax.broadcasted_iota(jnp.int32, (16, V), 0)
    chip_rows = jnp.where(lane == y * 16 + line, 1.0, 0.0).astype(BF16)
    rows_out = dot_nt(chip_rows, dressed)
    rows_out = jnp.concatenate([rows_out, jnp.zeros((16, V - Q), F32)], axis=1).astype(BF16)
    g_near[z] = rows_out
    for d in ORDER:
        send_earlier(slot_of(2, d), z_copy(d))

    loads[0].wait()
    loads[1].wait()
    lhs[pl.ds(0, Q * W), :] = gathered[:, core, NY - 1].reshape(Q * W, V)
    own_rows = jnp.where(lane == virt * W + line % W, 1.0, 0.0)
    fock_rows = dot_nt(own_rows.astype(BF16), fock[...])
    lhs[pl.ds(Q * W, 16), :] = jnp.where(line < W, fock_rows, own_rows).astype(BF16)

    def inter_step(jp, carry):
        both = dot_nt(lhs[...], amp[pl.ds(pl.multiple_of(jp * 2 * V, 2 * V), 2 * V), :])
        both = both.reshape(Q + 2, W, 2 * V)
        packed = jnp.concatenate([both[:, :, :V], both[:, :, V:]], axis=1).astype(BF16)
        inter[:, pl.ds(pl.multiple_of(jp * 16, 16), 16), :] = packed
        return carry

    for n in range(PARTS // 2, PARTS):
        amp_load(n).wait()
    part = NOCC // 8
    for n, group in enumerate(((1, 7), (2, 6), (3, 5), (4,))):
        lax.fori_loop(n * part, (n + 1) * part, inter_step, 0, unroll=8)
        for d in group:
            send_later(slot_of(1, d), y_copy(d))
    even = z % 2 == 0
    ensure(slot_of(0, 1))
    ensure(slot_of(0, 7))
    pl.when(even)(functools.partial(ensure, slot_of(2, 1)))
    pl.when(jnp.logical_not(even))(functools.partial(ensure, slot_of(2, 7)))
    for g in range(2):
        relay(g)

    split(1 - core)

    picked = []
    own_mat = own_rows.astype(BF16)
    for n in range(NOCC // 4):
        four = dot_nt(own_mat, ov_by_k[4 * n : 4 * n + 4].reshape(4 * Q, V))[:W]
        picked += [four[:, :V], four[:, V:]]
    picked = jnp.concatenate(picked, axis=0).astype(BF16)

    def twice(block):
        empty = jnp.zeros((Q, V), BF16)
        top = jnp.concatenate([block, empty], axis=1)
        return jnp.concatenate([top, jnp.concatenate([empty, block], axis=1)], axis=0)

    cycle = dot_nn(picked, twice(dressed)).reshape(NOCC // 2, W, 2 * V)
    cycle = jnp.concatenate([cycle[:, :, :V], cycle[:, :, V:]], axis=1).reshape(NOCC * W, V)
    half, number = pair // (NOCC // 2), pair % (NOCC // 2)
    ov_mine = ov_wide[pl.ds(half * (NOCC // 2 * Q) + number, Q, stride=NOCC // 2), :].astype(BF16)

    def ladder(quarter):
        first = pl.multiple_of(quarter % 4 * (Q // 4), Q // 4)
        for place in range(NY):
            chip = (y - (ORDER + (0,))[place]) % NY
            one, two = (gathered[quarter % 4, n, place].astype(F32).reshape(Q // 4, W, V) for n in range(2))
            both = jnp.concatenate([one, two], axis=1).astype(BF16)
            weights[pl.ds(first, Q // 4), pl.ds(pl.multiple_of(chip * 16, 16), 16), :] = both
        for m in range(0, NOCC * W, 256):
            part_sum = None
            for p in range(0, Q // 4, 2):
                left = [inter[first + p + n, m : m + 256] for n in range(2)]
                right = [weights[first + p + n] for n in range(2)]
                term = dot_nt(jnp.concatenate(left, axis=1), jnp.concatenate(right, axis=1))
                part_sum = term if part_sum is None else part_sum + term
            total[m : m + 256] += part_sum

    for m in range(0, NOCC * W, 256):
        fock_part = dot_nt(inter[Q + 1, m : m + 256], fock[...])
        total[m : m + 256] = fock_part + inter[Q, m : m + 256].astype(F32) + cycle[m : m + 256]
    other = gathered.at[:, 1 - core, NY - 1]
    remote(other, other, own_sem.at[0], own_sem.at[1], sibling).wait_recv()
    def plane_work():
        copies = []
        relay_in_plane(copies)
        for g in range(2):
            there = block(color, 1 - core, GROUPS[g])
            remote(there, there, in_send.at[g, 3], in_recv.at[g, 3], sibling).wait_recv()
        ladder(color)
        for n in (1, 0, 2):
            for g in range(2):
                there = block(color + 1 + n, 1 - core, GROUPS[g])
                remote(there, there, sib_send.at[g, n], sib_recv.at[g, n], sibling).wait_recv()
            ladder(color + 1 + n)
        for copy in copies:
            copy.wait_send()

    def to_leader(d):
        return later[slot_of(2, d)] & (z + d == NZ)

    def serve(d, ensured):
        if not ensured:
            pl.semaphore_wait(ready.at[slot_of(2, d)], 1)
        z_copy(d).start()

    for d in (5, 6, 7):
        pl.when(to_leader(d))(functools.partial(serve, d, d == 7))
    pl.when(jnp.logical_not(even))(functools.partial(ensure, slot_of(2, 1)))
    pl.when(even)(functools.partial(ensure, slot_of(2, 7)))
    for d in range(1, NZ):
        others = later[slot_of(2, d)] & (z + d != NZ)
        pl.when(others)(functools.partial(serve, d, d in (1, 7)))
        sends.append((later[slot_of(2, d)], z_copy(d)))

    for d in range(1, NZ):
        there = g_near.at[(z - d) % NZ]
        remote(there, there, g_sem.at[0, d - 1], g_sem.at[1, d - 1], sibling).wait_recv()

    def near_rows(n):
        wide = g_near[n].astype(F32)
        return jnp.where(core == 0, wide[:W], wide[W:])

    for m in range(NZ // 2):
        low, high = near_rows(m), near_rows(m + NZ // 2)
        both = jnp.concatenate([low[:, :Q], high[:, :Q]], axis=1)
        g_pack[pl.ds(m * W, W), :] = both
    g_far[x] = g_pack[...].astype(BF16)
    for d in range(2, NX - 1):
        ensure(slot_of(0, d))
    for d in range(1, NX):
        start(remote(g_far.at[x], g_far.at[x], g_sem.at[2, d - 1], g_sem.at[3, d - 1], peers[slot_of(0, d)]))

    plane_work()

    drain()
    for d in range(1, NX):
        there = g_far.at[(x - d) % NX]
        remote(there, there, g_sem.at[2, d - 1], g_sem.at[3, d - 1], sibling).wait_recv()
    mirror = dot_nn(g_far[...].reshape(NX * NZ // 2 * W, V), twice(ov_mine))
    mirror = mirror.reshape(NX, NZ // 2, W, 2 * V)

    loads[2].wait()
    for j in range(0, NOCC, 2):
        tiles = []
        for k in (j, j + 1):
            jx, jz = k // NZ, k % NZ
            lanes = slice(jz // (NZ // 2) * V, (jz // (NZ // 2) + 1) * V)
            tile = total[k * W : (k + 1) * W] + mirror[jx, jz % (NZ // 2), :, lanes]
            tiles.append(tile * screen[0, k].astype(F32))
        out_ref[pl.ds(j * W, 16), :] = jnp.concatenate(tiles, axis=0).astype(BF16)

    drain()


def body(amplitudes, factors, ov_factors, fock_matrix, screen):
    vmem, dma = pltpu.VMEM, pltpu.SemaphoreType.DMA
    out = pl.pallas_call(
        kernel,
        out_shape=jax.ShapeDtypeStruct((NOCC * W, V), BF16),
        in_specs=[pl.BlockSpec(memory_space=pl.ANY)] * 5,
        out_specs=pl.BlockSpec(memory_space=pltpu.VMEM),
        scratch_shapes=[
            vmem((NOCC * V, V), BF16),
            vmem((Q, NOCC, V), BF16),
            vmem((Q * NOCC, V), F32),
            vmem((NOCC, Q, V), BF16),
            vmem((V, V), BF16),
            pltpu.SMEM((1, NOCC), jnp.int32),
            vmem(((Q + 2) * W, V), BF16),
            vmem((4, 2, NY, QROWS, V), BF16),
            vmem((Q + 2, NOCC * W, V), BF16),
            vmem((Q, V, V), BF16),
            vmem((NOCC * W, V), F32),
            vmem((2, Q, V), F32),
            vmem((NX, 16, V), BF16),
            vmem((NX // 2 * W, V), F32),
            vmem((NX, NZ // 2 * W, V), BF16),
            dma((6,)),
            dma((2,)),
            dma((PARTS,)),
            dma((2,)),
            dma((NY - 1,)),
            dma((NY - 1,)),
            dma((2, 4)),
            dma((2, 4)),
            dma((2, 3)),
            dma((2, 3)),
            dma((2,)),
            dma((4, NX - 1)),
            pltpu.SemaphoreType.REGULAR((22,)),
        ],
        compiler_params=pltpu.CompilerParams(
            collective_id=0, has_side_effects=True, vmem_limit_bytes=62 * 1024 * 1024
        ),
        name="residual",
    )(
        amplitudes.reshape(NOCC * V, V),
        factors.reshape(4, QROWS, V),
        ov_factors,
        fock_matrix,
        screen,
    )
    return out.reshape(NOCC, W, V)


def solution(mesh):
    in_specs = (P("pair", None, None), P(None, "virt", None), P(), P(), P("pair", None))
    out_specs = P("pair", "virt", None)
    return jax.shard_map(body, mesh=mesh, in_specs=in_specs, out_specs=out_specs, check_vma=False)
```

time: 36.1 us -> 35.4 us (0.981)
  Pallas kernels: 34.2 us -> 33.7 us
    pallas_call x1, Pallas kernels: 34.2 us -> 33.7 us  [body(): pl.pallas_call(kernel, out_shape=jax.ShapeDtypeStruct((NOCC * W, V), BF16...]
where the time goes in v4:
time: 35.4 us; the launch traced here: 35.3 us
  Pallas kernels  33.7 us (95%)
  local copies, waits for them, and re-layouts  1.57 us (4%)
    pallas_call x1, Pallas kernels, body(): pl.pallas_call(kernel, out_shape=jax.ShapeDtypeStruct((NOCC * W, V), BF16...  33.7 us
    unnamed x1, local copies, waits for them, and re-layouts  1.57 us

profile of v4, /device:TPU:1, one launch (start us, length us, event | category | flops | bytes accessed | tf_op | source)
XLA Modules:
  0.0 35.3 jit_solution(14157146528086828086)
XLA Ops:
  0.0 33.7 %residual.1 = bf16[512,128]{1,0:T(8,128)(2,1)} custom-call(bf16[8192,128]{1,0:T(8,128)(2,1)} %bitcast.3, bf16[4,128,128]{2,1,0:T(8,128)(2,1)} %bitcast.5, bf16[64,64,128]{2,1,0:T(8,128)(2,1)} %ov_hbm.1, bf16[128,128]{1,0:T(8,128)(2,1)} %fock_hbm.1, s32[1,64]{1,0:T(1,128)} %screen_hbm.1), custom_call_target="tpu_custom_call" | custom-call | tf_op jit(solution)/shard_map/residual/pallas_call | solution.py:360
  33.7 1.6 %copy.7 = bf16[64,8,128]{2,1,0:T(8,128)(2,1)} copy(bf16[64,8,128]{2,1,0:T(8,128)(2,1)} %bitcast.4) | data formatting | bytes 262144

commit v5 on v4

--- a/solution.py
+++ b/solution.py
@@ -129,13 +129,16 @@
             start(remote(piece, piece, in_send.at[g, way], in_recv.at[g, way], (target, virt)))
         start(remote(piece, piece, in_send.at[g, 3], in_recv.at[g, 3], sibling))
 
-    def relay_in_plane(copies):
+    def relay_in_plane(g, copies):
         for n, way in ((1, 2), (0, 1), (2, 0)):
-            for g in range(2):
-                piece = block(color + 1 + n, core, GROUPS[g])
-                remote(piece, piece, in_send.at[g, way], in_recv.at[g, way], sibling).wait_recv()
-                copies.append(remote(piece, piece, sib_send.at[g, n], sib_recv.at[g, n], sibling))
-                copies[-1].start()
+            piece = block(color + 1 + n, core, GROUPS[g])
+            remote(piece, piece, in_send.at[g, way], in_recv.at[g, way], sibling).wait_recv()
+            copies[n].start()
+
+    to_sibling = []
+    for g in range(2):
+        pieces = [block(color + 1 + n, core, GROUPS[g]) for n in range(3)]
+        to_sibling.append([remote(p, p, sib_send.at[g, n], sib_recv.at[g, n], sibling) for n, p in enumerate(pieces)])
 
     def y_copy(d):
         place = ORDER.index(d)
@@ -284,8 +287,8 @@
     other = gathered.at[:, 1 - core, NY - 1]
     remote(other, other, own_sem.at[0], own_sem.at[1], sibling).wait_recv()
     def plane_work():
-        copies = []
-        relay_in_plane(copies)
+        pl.when(z > 0)(functools.partial(relay_in_plane, 0, to_sibling[0]))
+        relay_in_plane(1, to_sibling[1])
         for g in range(2):
             there = block(color, 1 - core, GROUPS[g])
             remote(there, there, in_send.at[g, 3], in_recv.at[g, 3], sibling).wait_recv()
@@ -295,8 +298,10 @@
                 there = block(color + 1 + n, 1 - core, GROUPS[g])
                 remote(there, there, sib_send.at[g, n], sib_recv.at[g, n], sibling).wait_recv()
             ladder(color + 1 + n)
-        for copy in copies:
+        for copy in to_sibling[0] + to_sibling[1]:
             copy.wait_send()
+
+    pl.when(z == 0)(functools.partial(relay_in_plane, 0, to_sibling[0]))
 
     def to_leader(d):
         return later[slot_of(2, d)] & (z + d == NZ)

time: 35.4 us -> 35.3 us (level)
  no operation moved by 1% of the time
where the time goes in v5:
time: 35.3 us; the launch traced here: 35.1 us
  Pallas kernels  33.5 us (95%)
  local copies, waits for them, and re-layouts  1.57 us (4%)
    pallas_call x1, Pallas kernels, body(): pl.pallas_call(kernel, out_shape=jax.ShapeDtypeStruct((NOCC * W, V), BF16...  33.5 us
    unnamed x1, local copies, waits for them, and re-layouts  1.57 us

profile of v5, /device:TPU:1, one launch (start us, length us, event | category | flops | bytes accessed | tf_op | source)
XLA Modules:
  0.0 35.1 jit_solution(3569533555953423055)
XLA Ops:
  0.0 33.5 %residual.1 = bf16[512,128]{1,0:T(8,128)(2,1)} custom-call(bf16[8192,128]{1,0:T(8,128)(2,1)} %bitcast.3, bf16[4,128,128]{2,1,0:T(8,128)(2,1)} %bitcast.5, bf16[64,64,128]{2,1,0:T(8,128)(2,1)} %ov_hbm.1, bf16[128,128]{1,0:T(8,128)(2,1)} %fock_hbm.1, s32[1,64]{1,0:T(1,128)} %screen_hbm.1), custom_call_target="tpu_custom_call" | custom-call | tf_op jit(solution)/shard_map/residual/pallas_call | solution.py:365
  33.6 1.6 %copy.7 = bf16[64,8,128]{2,1,0:T(8,128)(2,1)} copy(bf16[64,8,128]{2,1,0:T(8,128)(2,1)} %bitcast.4) | data formatting | bytes 262144
